TPU v7x, 32 devices: a whole 2x2x4 slice. The times are simulated.
32 devices in a mesh: groups: 2 (over y), expert: 4 (over z), section: 4 (over x, core).
Axes of the slice: x: 2, y: 2, z: 4, core: 2. Of those that a mesh axis runs over, the one named last changes fastest.
Arguments:
- pending_microgroups: bfloat16 [4, 1024, 768], P('section', ('groups', 'expert')), parts along dimension 1, may hold values from -6 to 6
- arriving_microgroups: bfloat16 [2, 1024, 768], P(None, ('groups', 'expert')), parts along dimension 1, may hold values from -6 to 6
- expert_choice_grid: int32 [3, 4, 1024], P(None, 'section', ('groups', 'expert')), parts along dimension 2, may hold values from 0 to 1, as said below
- rootmean_gain: float32 [4, 768], P('section'), may hold values from 0.5 to 1.5
- gating_columns: bfloat16 [4, 768, 2], P('section'), may hold values from -0.21875 to 0.21875
- up_projection_matrix: bfloat16 [4, 4, 768, 768], P('section', 'expert'), may hold values from -0.21875 to 0.21875
- down_projection_matrix: bfloat16 [4, 4, 768, 768], P('section', 'expert'), may hold values from -0.21875 to 0.21875
Outputs:
- section_out: bfloat16 [4, 3, 1024, 768], P('section', None, ('groups', 'expert')), parts along dimension 2
There are 2 independent parts, one for each index of `groups`. A program takes and returns all parts, laid end to end along the dimension named above; an argument that names none is the same for every part. Nothing has to cross between parts.
Inputs may be any that keep to these rules, and one draw needn't show every extreme that they name: `expert_choice_grid`: for every tick and section, no expert is named by more than 128 tokens of one aligned block of 128 tokens (the tokens of one device), and one expert, drawn from the seed, is named by exactly 128 tokens of every such block.
All inputs are finite; a program needn't handle non-finite values.
Results may differ from a plain program's by a relative error of at most 0.0095.
Values may be sent and summed in bfloat16 or wider, within the bound.
A program may use at most 64 MiB of HBM per device.

v0:
```python
import jax
import jax.numpy as jnp
from jax import lax
from jax.sharding import PartitionSpec as P

TICKS = 3


def swapped(x, axis, bit):
    return lax.ppermute(x, axis, [(i, i ^ 1 << bit) for i in range(lax.axis_size(axis))])


def from_behind(value, axis, steps):
    count = lax.axis_size(axis)
    initial, last = (max(0, -steps), min(count, count - steps))
    return lax.ppermute(value, axis, [(source, source + steps) for source in range(initial, last)])


def half_output(received, up_projection_matrix, down_projection_matrix):
    hidden = jnp.maximum(
        jnp.einsum(
            "sid,dh->sih", received, up_projection_matrix, preferred_element_type=jnp.float32
        ),
        0.0,
    ).astype(jnp.bfloat16)
    return jnp.einsum(
        "sih,hd->sid", hidden, down_projection_matrix, preferred_element_type=jnp.float32
    ).astype(jnp.bfloat16)


def expert_layer(
    tok_rows,
    routes,
    rootmean_gain,
    gating_columns,
    up_projection_matrix,
    down_projection_matrix,
    other_in,
    other_out,
):
    num_rows, width = tok_rows.shape
    experts = gating_columns.shape[1]
    capacity = min(num_rows, 3 * num_rows // experts)
    float_rows = tok_rows.astype(jnp.float32)
    inv_rms = lax.rsqrt(jnp.mean(float_rows * float_rows, axis=-1, keepdims=True) + 1e-06)
    normed = (float_rows * inv_rms * rootmean_gain).astype(jnp.bfloat16)
    logits = jnp.dot(normed, gating_columns, preferred_element_type=jnp.float32)
    one_hot = routes[:, None] == jnp.arange(experts, dtype=jnp.int32)[None, :]
    gate_value = jax.nn.sigmoid(jnp.sum(jnp.where(one_hot, logits, 0.0), axis=1))
    flags = one_hot.astype(jnp.int32)
    slot_rank = jnp.sum((jnp.cumsum(flags, axis=0) - flags) * flags, axis=1)
    slot_index = routes * capacity + slot_rank
    placing = (
        slot_index[None, :] == jnp.arange(experts * capacity, dtype=jnp.int32)[:, None]
    ).astype(jnp.bfloat16)
    outgoing = jnp.dot(placing, normed, preferred_element_type=jnp.float32).astype(jnp.bfloat16)
    outgoing = outgoing.reshape(experts, capacity, width)
    halves = outgoing.reshape(2 * experts, capacity // 2, width)
    received = lax.all_to_all(halves, "expert", split_axis=0, concat_axis=0, tiled=True)
    own_part = half_output(received, up_projection_matrix, down_projection_matrix)
    other_part = half_output(received, other_in, other_out)
    summed = (own_part.astype(jnp.float32) + other_part.astype(jnp.float32)).astype(jnp.bfloat16)
    combined = lax.all_to_all(summed, "expert", split_axis=0, concat_axis=0, tiled=True)
    flat_out = combined.reshape(experts * capacity, width)
    expert_out = lax.dot_general(
        placing, flat_out, (((0,), (0,)), ((), ())), preferred_element_type=jnp.float32
    )
    return (float_rows + gate_value[:, None] * expert_out).astype(jnp.bfloat16)


def per_device(
    pending_microgroups,
    arriving_microgroups,
    expert_choice_grid,
    rootmean_gain,
    gating_columns,
    up_projection_matrix,
    down_projection_matrix,
):
    leg_position = lax.axis_index("section")
    own_in = up_projection_matrix[0, 0]
    own_out = down_projection_matrix[0, 0]
    other_in, other_out = swapped((own_in, own_out), "expert", 0)
    running_activation = pending_microgroups[0]
    per_tick = []
    for tick_idx in range(TICKS):
        layer_out = expert_layer(
            running_activation,
            expert_choice_grid[tick_idx, 0],
            rootmean_gain[0],
            gating_columns[0],
            own_in,
            own_out,
            other_in,
            other_out,
        )
        per_tick.append(layer_out)
        if tick_idx + 1 < TICKS:
            moved = from_behind(layer_out, "section", 1)
            running_activation = jnp.where(leg_position == 0, arriving_microgroups[tick_idx], moved)
    return jnp.stack(per_tick)[None]


def solution(mesh):
    placed = (
        P("section", ("groups", "expert"), None),
        P(None, ("groups", "expert"), None),
        P(None, "section", ("groups", "expert")),
        P("section", None),
        P("section", None, None),
        P("section", "expert", None, None),
        P("section", "expert", None, None),
    )
    return jax.shard_map(
        per_device,
        mesh=mesh,
        in_specs=placed,
        out_specs=P("section", None, ("groups", "expert"), None),
        check_vma=False,
    )
```

profile of v0, /device:TPU:0, one launch (start us, length us, event | category | flops | bytes accessed | tf_op | source)
XLA Modules:
  0.0 162.1 jit_solution(12954979192620634909)
XLA Ops:
  0.0 3.0 %collective-permute-start.1 = (bf16[768,768]{1,0:T(8,128)(2,1)}, bf16[768,768]{1,0:T(8,128)(2,1)}, u32[]{:S(2)}, u32[]{:S(2)}) collective-permute-start(bf16[768,768]{1,0:T(8,128)(2,1)} %bitcast.110), channel_id=1, source_target_pairs={{0,4},{4,0},{8,12},{12,8},{1,5},{5,1},{9,13},{13,9},{2,6},{6,2},{1... | collective-permute-start | bytes 3538952 | tf_op jit(solution)/shard_map/ppermute | solution.py:10
  3.1 1.2 fusion.48
  6.9 0.7 reduce
  7.6 1.3 convolution_convert_fusion.8
  8.8 53.5 %all_to_all.30 = bf16[4,64,768]{2,1,0:T(8,128)(2,1)S(1)} all-to-all(bf16[4,64,768]{2,1,0:T(8,128)(2,1)S(1)} %bitcast.105), channel_id=1, replica_groups=mesh['groups'=2,'expert'=4,'section'=4] {'expert'}, dimensions={0} | all-to-all | bytes 786432 | tf_op jit(solution)/shard_map/all_to_all | solution.py:59
  62.3 1.8 %fusion.17 = f32[4,64,768]{2,1,0:T(8,128)} fusion(bf16[4,64,768]{2,1,0:T(8,128)(2,1)S(1)} %all_to_all.30, bf16[1,1,768,768]{3,2,1,0:T(8,128)(2,1)S(1)} %copy-done.3, bf16[1,1,768,768]{3,2,1,0:T(8,128)(2,1)S(1)} %copy-done.4), kind=kOutput, calls=%fused_computation.31 | convolution fusion | flops 604766208 | bytes 3538944 | tf_op jit(solution)/shard_map/sih,hd->sid/dot_general | solution.py:26
  64.1 3.5 %fusion.16 = bf16[4,64,768]{2,1,0:T(8,128)(2,1)} fusion(f32[4,64,768]{2,1,0:T(8,128)} %fusion.17, bf16[4,64,768]{2,1,0:T(8,128)(2,1)S(1)} %all_to_all.30, bf16[768,768]{1,0:T(8,128)(2,1)} %collective-permute-done.1, bf16[768,768]{1,0:T(8,128)(2,1)} %collective-permute-done), kind=kOutput, calls=%fused_computation.29 | convolution fusion | flops 605159424 | bytes 3932160 | tf_op jit(solution)/shard_map/sih,hd->sid/dot_general | solution.py:26
  67.7 3.7 %all-to-all-start.1 = ((bf16[4,64,768]{2,1,0:T(8,128)(2,1)}), bf16[4,64,768]{2,1,0:T(8,128)(2,1)S(1)}, u32[]{:S(2)}, u32[]{:S(2)}) async-start(bf16[4,64,768]{2,1,0:T(8,128)(2,1)} %fusion.16), calls=%async_computation.1 | async-start | bytes 786432 | tf_op jit(solution)/shard_map/all_to_all | solution.py:63
  71.6 10.3 %all-to-all-done.1 = bf16[4,64,768]{2,1,0:T(8,128)(2,1)S(1)} async-done(((bf16[4,64,768]{2,1,0:T(8,128)(2,1)}), bf16[4,64,768]{2,1,0:T(8,128)(2,1)S(1)}, u32[]{:S(2)}, u32[]{:S(2)}) %all-to-all-start.1) | async-done | bytes 393248 | tf_op jit(solution)/shard_map/all_to_all | solution.py:63
  82.2 1.3 collective-permute-start.2
  83.5 1.0 collective-permute-done.2
  85.0 12.9 %all_to_all.31 = bf16[4,64,768]{2,1,0:T(8,128)(2,1)S(1)} all-to-all(bf16[4,64,768]{2,1,0:T(8,128)(2,1)S(1)} %bitcast.106), channel_id=1, replica_groups=mesh['groups'=2,'expert'=4,'section'=4] {'expert'}, dimensions={0} | all-to-all | bytes 786432 | tf_op jit(solution)/shard_map/all_to_all | solution.py:59
  97.9 2.2 %fusion.13 = f32[4,64,768]{2,1,0:T(8,128)S(1)} fusion(bf16[4,64,768]{2,1,0:T(8,128)(2,1)S(1)} %all_to_all.31, bf16[1,1,768,768]{3,2,1,0:T(8,128)(2,1)S(1)} %copy-done.3, bf16[1,1,768,768]{3,2,1,0:T(8,128)(2,1)} %param.12), kind=kOutput, calls=%fused_computation.24 | convolution fusion | flops 604766208 | bytes 3538944 | tf_op jit(solution)/shard_map/sih,hd->sid/dot_general | solution.py:26
  100.1 3.3 %fusion.12 = bf16[4,64,768]{2,1,0:T(8,128)(2,1)} fusion(f32[4,64,768]{2,1,0:T(8,128)S(1)} %fusion.13, bf16[4,64,768]{2,1,0:T(8,128)(2,1)S(1)} %all_to_all.31, bf16[768,768]{1,0:T(8,128)(2,1)} %collective-permute-done.1, bf16[768,768]{1,0:T(8,128)(2,1)} %collective-permute-done), kind=kOutput, calls=%fused_computation.22 | convolution fusion | flops 605159424 | bytes 3932160 | tf_op jit(solution)/shard_map/sih,hd->sid/dot_general | solution.py:26
  103.4 4.4 %all-to-all-start.3 = ((bf16[4,64,768]{2,1,0:T(8,128)(2,1)}), bf16[4,64,768]{2,1,0:T(8,128)(2,1)S(1)}, u32[]{:S(2)}, u32[]{:S(2)}) async-start(bf16[4,64,768]{2,1,0:T(8,128)(2,1)} %fusion.12), calls=%async_computation.3 | async-start | bytes 786432 | tf_op jit(solution)/shard_map/all_to_all | solution.py:63
  108.1 12.2 %all-to-all-done.3 = bf16[4,64,768]{2,1,0:T(8,128)(2,1)S(1)} async-done(((bf16[4,64,768]{2,1,0:T(8,128)(2,1)}), bf16[4,64,768]{2,1,0:T(8,128)(2,1)S(1)}, u32[]{:S(2)}, u32[]{:S(2)}) %all-to-all-start.3) | async-done | bytes 393248 | tf_op jit(solution)/shard_map/all_to_all | solution.py:63
  120.6 2.3 %collective-permute-start.3 = (bf16[128,768]{1,0:T(8,128)(2,1)S(1)}, bf16[128,768]{1,0:T(8,128)(2,1)S(1)}, u32[]{:S(2)}, u32[]{:S(2)}) collective-permute-start(bf16[128,768]{1,0:T(8,128)(2,1)S(1)} %fusion.40), channel_id=1, source_target_pairs={{0,1},{1,2},{2,3},{4,5},{5,6},{6,7},{8,9},{9,10},{10,11},{12,13},{... | collective-permute-start | bytes 589832 | tf_op jit(solution)/shard_map/ppermute | solution.py:16
  122.9 1.0 collective-permute-done.3
  124.4 15.3 %all_to_all.32 = bf16[4,64,768]{2,1,0:T(8,128)(2,1)S(1)} all-to-all(bf16[4,64,768]{2,1,0:T(8,128)(2,1)S(1)} %bitcast.107), channel_id=1, replica_groups=mesh['groups'=2,'expert'=4,'section'=4] {'expert'}, dimensions={0} | all-to-all | bytes 786432 | tf_op jit(solution)/shard_map/all_to_all | solution.py:59
  139.7 2.2 %fusion.9 = f32[4,64,768]{2,1,0:T(8,128)S(1)} fusion(bf16[4,64,768]{2,1,0:T(8,128)(2,1)S(1)} %all_to_all.32, bf16[1,1,768,768]{3,2,1,0:T(8,128)(2,1)S(1)} %copy-done.3, bf16[1,1,768,768]{3,2,1,0:T(8,128)(2,1)} %param.12), kind=kOutput, calls=%fused_computation.17 | convolution fusion | flops 604766208 | bytes 3538944 | tf_op jit(solution)/shard_map/sih,hd->sid/dot_general | solution.py:26
  141.9 3.3 %fusion.8 = bf16[4,64,768]{2,1,0:T(8,128)(2,1)} fusion(f32[4,64,768]{2,1,0:T(8,128)S(1)} %fusion.9, bf16[4,64,768]{2,1,0:T(8,128)(2,1)S(1)} %all_to_all.32, bf16[768,768]{1,0:T(8,128)(2,1)} %collective-permute-done.1, bf16[768,768]{1,0:T(8,128)(2,1)} %collective-permute-done), kind=kOutput, calls=%fused_computation.15 | convolution fusion | flops 605159424 | bytes 3932160 | tf_op jit(solution)/shard_map/sih,hd->sid/dot_general | solution.py:26
  145.2 3.5 %all-to-all-start.5 = ((bf16[4,64,768]{2,1,0:T(8,128)(2,1)}), bf16[4,64,768]{2,1,0:T(8,128)(2,1)S(1)}, u32[]{:S(2)}, u32[]{:S(2)}) async-start(bf16[4,64,768]{2,1,0:T(8,128)(2,1)} %fusion.8), calls=%async_computation.5 | async-start | bytes 786432 | tf_op jit(solution)/shard_map/all_to_all | solution.py:63
  148.9 12.0 %all-to-all-done.5 = bf16[4,64,768]{2,1,0:T(8,128)(2,1)S(1)} async-done(((bf16[4,64,768]{2,1,0:T(8,128)(2,1)}), bf16[4,64,768]{2,1,0:T(8,128)(2,1)S(1)}, u32[]{:S(2)}, u32[]{:S(2)}) %all-to-all-start.5) | async-done | bytes 393248 | tf_op jit(solution)/shard_map/all_to_all | solution.py:63
  161.2 0.9 maximum_bitcast_fusion
  (45 shorter events, 5.2 us)
Async XLA Ops:
  0.0 71.3 %copy-start = (bf16[1,768,2]{1,2,0:T(2,128)(2,1)S(1)}, bf16[1,768,2]{1,2,0:T(2,128)(2,1)}, u32[]{:S(2)}) copy-start(bf16[1,768,2]{1,2,0:T(2,128)(2,1)} %param.11) | copy-start | bytes 9220
  0.0 64.1 %collective-permute-start.1 = (bf16[768,768]{1,0:T(8,128)(2,1)}, bf16[768,768]{1,0:T(8,128)(2,1)}, u32[]{:S(2)}, u32[]{:S(2)}) collective-permute-start(bf16[768,768]{1,0:T(8,128)(2,1)} %bitcast.110), channel_id=1, source_target_pairs={{0,4},{4,0},{8,12},{12,8},{1,5},{5,1},{9,13},{13,9},{2,6},{6,2},{1... | collective-permute-start | bytes 3538952 | tf_op jit(solution)/shard_map/ppermute | solution.py:10
  3.0 59.3 %copy-start.3 = (bf16[1,1,768,768]{3,2,1,0:T(8,128)(2,1)S(1)}, bf16[1,1,768,768]{3,2,1,0:T(8,128)(2,1)}, u32[]{:S(2)}) copy-start(bf16[1,1,768,768]{3,2,1,0:T(8,128)(2,1)} %param.13) | copy-start | bytes 3538948
  3.0 59.3 %copy-start.4 = (bf16[1,1,768,768]{3,2,1,0:T(8,128)(2,1)S(1)}, bf16[1,1,768,768]{3,2,1,0:T(8,128)(2,1)}, u32[]{:S(2)}) copy-start(bf16[1,1,768,768]{3,2,1,0:T(8,128)(2,1)} %param.12) | copy-start | bytes 3538948
  3.0 61.1 %collective-permute-start = (bf16[768,768]{1,0:T(8,128)(2,1)}, bf16[768,768]{1,0:T(8,128)(2,1)}, u32[]{:S(2)}, u32[]{:S(2)}) collective-permute-start(bf16[768,768]{1,0:T(8,128)(2,1)} %bitcast.111), channel_id=1, source_target_pairs={{0,4},{4,0},{8,12},{12,8},{1,5},{5,1},{9,13},{13,9},{2,6},{6,2},{1... | collective-permute-start | bytes 3538952 | tf_op jit(solution)/shard_map/ppermute | solution.py:10
  64.1 7.2 %copy-start.1 = (bf16[1,128,768]{2,1,0:T(8,128)(2,1)S(1)}, bf16[1,128,768]{2,1,0:T(8,128)(2,1)}, u32[]{:S(2)}) copy-start(bf16[1,128,768]{2,1,0:T(8,128)(2,1)} %param.7) | copy-start | bytes 589828
  67.7 16.9 %copy-start.2 = (bf16[2,128,768]{2,1,0:T(8,128)(2,1)S(1)}, bf16[2,128,768]{2,1,0:T(8,128)(2,1)}, u32[]{:S(2)}) copy-start(bf16[2,128,768]{2,1,0:T(8,128)(2,1)} %param.8) | copy-start | bytes 1179652
  67.7 14.2 %all-to-all-start.1 = ((bf16[4,64,768]{2,1,0:T(8,128)(2,1)}), bf16[4,64,768]{2,1,0:T(8,128)(2,1)S(1)}, u32[]{:S(2)}, u32[]{:S(2)}) async-start(bf16[4,64,768]{2,1,0:T(8,128)(2,1)} %fusion.16), calls=%async_computation.1 | async-start | bytes 786432 | tf_op jit(solution)/shard_map/all_to_all | solution.py:63
  82.2 2.4 %collective-permute-start.2 = (bf16[128,768]{1,0:T(8,128)(2,1)S(1)}, bf16[128,768]{1,0:T(8,128)(2,1)S(1)}, u32[]{:S(2)}, u32[]{:S(2)}) collective-permute-start(bf16[128,768]{1,0:T(8,128)(2,1)S(1)} %fusion.41), channel_id=1, source_target_pairs={{0,1},{1,2},{2,3},{4,5},{5,6},{6,7},{8,9},{9,10},{10,11},{12,13},{... | collective-permute-start | bytes 589832 | tf_op jit(solution)/shard_map/ppermute | solution.py:16
  103.4 16.9 %all-to-all-start.3 = ((bf16[4,64,768]{2,1,0:T(8,128)(2,1)}), bf16[4,64,768]{2,1,0:T(8,128)(2,1)S(1)}, u32[]{:S(2)}, u32[]{:S(2)}) async-start(bf16[4,64,768]{2,1,0:T(8,128)(2,1)} %fusion.12), calls=%async_computation.3 | async-start | bytes 786432 | tf_op jit(solution)/shard_map/all_to_all | solution.py:63
  120.6 3.4 %collective-permute-start.3 = (bf16[128,768]{1,0:T(8,128)(2,1)S(1)}, bf16[128,768]{1,0:T(8,128)(2,1)S(1)}, u32[]{:S(2)}, u32[]{:S(2)}) collective-permute-start(bf16[128,768]{1,0:T(8,128)(2,1)S(1)} %fusion.40), channel_id=1, source_target_pairs={{0,1},{1,2},{2,3},{4,5},{5,6},{6,7},{8,9},{9,10},{10,11},{12,13},{... | collective-permute-start | bytes 589832 | tf_op jit(solution)/shard_map/ppermute | solution.py:16
  145.2 15.8 %all-to-all-start.5 = ((bf16[4,64,768]{2,1,0:T(8,128)(2,1)}), bf16[4,64,768]{2,1,0:T(8,128)(2,1)S(1)}, u32[]{:S(2)}, u32[]{:S(2)}) async-start(bf16[4,64,768]{2,1,0:T(8,128)(2,1)} %fusion.8), calls=%async_computation.5 | async-start | bytes 786432 | tf_op jit(solution)/shard_map/all_to_all | solution.py:63
where the time goes:
time: 163 us; the launch traced here: 162 us
  blocking collectives  81.6 us (50%)
  waiting for transfers between devices  36.6 us (22%)
  matrix products  19.6 us (12%)
  starting transfers between devices  18.2 us (11%)
  other arithmetic  4.56 us (3%)
    all_to_all x3, blocking collectives, expert_layer(): lax.all_to_all(halves, 'expert', split_axis=0, concat_axis=0, tiled=True)  81.6 us
    all_to_all x3, waiting for transfers between devices, expert_layer(): lax.all_to_all(summed, 'expert', split_axis=0, concat_axis=0, tiled=True)  34.5 us
    dot_general x6, matrix products, half_output(): jnp.einsum('sih,hd->sid', hidden, down_projection_matrix, preferred_eleme...  16.3 us
    all_to_all x3, starting transfers between devices, expert_layer(): lax.all_to_all(summed, 'expert', split_axis=0, concat_axis=0, tiled=True)  11.5 us
    ppermute x2, starting transfers between devices, from_behind(): lax.ppermute(value, axis, [(source, source + steps) for source in range(i...  3.62 us
  transfers between devices with their start and end apart: 7, of which 5 were waited for; matrix products, arithmetic and copies ran while one was open for 5% of the time, Pallas kernels for 0%

commit v1 on v0

--- a/solution.py
+++ b/solution.py
@@ -1,6 +1,10 @@
+import functools
+
 import jax
 import jax.numpy as jnp
 from jax import lax
+from jax.experimental import pallas as pl
+from jax.experimental.pallas import tpu as pltpu
 from jax.sharding import PartitionSpec as P
 
 TICKS = 3
@@ -47,8 +51,9 @@
     logits = jnp.dot(normed, gating_columns, preferred_element_type=jnp.float32)
     one_hot = routes[:, None] == jnp.arange(experts, dtype=jnp.int32)[None, :]
     gate_value = jax.nn.sigmoid(jnp.sum(jnp.where(one_hot, logits, 0.0), axis=1))
-    flags = one_hot.astype(jnp.int32)
-    slot_rank = jnp.sum((jnp.cumsum(flags, axis=0) - flags) * flags, axis=1)
+    order = jnp.arange(num_rows, dtype=jnp.int32)
+    same_before = (routes[:, None] == routes[None, :]) & (order[:, None] > order[None, :])
+    slot_rank = jnp.sum(same_before.astype(jnp.int32), axis=1)
     slot_index = routes * capacity + slot_rank
     placing = (
         slot_index[None, :] == jnp.arange(experts * capacity, dtype=jnp.int32)[:, None]
@@ -101,6 +106,352 @@
     return jnp.stack(per_tick)[None]
 
 
+MESH = pl.DeviceIdType.MESH
+IN_FLIGHT = 3
+
+
+def column_of(row):
+    count = row.shape[1]
+    down = lax.broadcasted_iota(jnp.int32, (count, count), 0)
+    along = lax.broadcasted_iota(jnp.int32, (count, count), 1)
+    return jnp.sum(jnp.where(down == along, row, 0.0), axis=1, keepdims=True)
+
+
+def relay_kernel(
+    sections,
+    cut,
+    pending,
+    arriving,
+    routes,
+    gain,
+    gating,
+    up,
+    down,
+    out,
+    x,
+    part,
+    their_part,
+    y_out,
+    ids,
+    own_up,
+    own_down,
+    far_up,
+    far_down,
+    own_sum,
+    hidden,
+    gate,
+    load_sem,
+    x_sem,
+    up_sem,
+    up_share_sem,
+    down_sem,
+    down_share_sem,
+    part_sem,
+    relay_sem,
+):
+    ticks = out.shape[1]
+    rows, width = out.shape[2:]
+    hid = up.shape[3]
+    up_cut = up_sem.shape[1]
+    group = lax.axis_index("groups")
+    place = lax.axis_index("expert")
+    section = lax.axis_index("section")
+    slot = lax.rem(place, 2)
+    own_expert = place // 2
+    mate = {"expert": place + 1 - 2 * slot}
+    across = {"expert": lax.rem(place + 2, 4)}
+    twin = {"groups": 1 - group}
+    ahead = {"section": jnp.minimum(section + 1, sections - 1)}
+    behind = {"section": jnp.maximum(section - 1, 0)}
+    first = section == 0
+    has_ahead = section < sections - 1
+    has_behind = section > 0
+
+    def remote(source, target, sems, index, device):
+        return pltpu.make_async_remote_copy(
+            src_ref=source,
+            dst_ref=target,
+            send_sem=sems.at[(0, *index)],
+            recv_sem=sems.at[(1, *index)],
+            device_id=device,
+            device_id_type=MESH,
+        )
+
+    half = width // 2
+    my_half = pl.multiple_of(group * half, half)
+    twin_half = pl.multiple_of((1 - group) * half, half)
+    hid_half = hid // 2
+    my_hid = pl.multiple_of(group * hid_half, hid_half)
+    twin_hid = pl.multiple_of((1 - group) * hid_half, hid_half)
+    wide = width // cut
+    piece = half // up_cut
+
+    def up_rows(begin, k):
+        return pl.ds(pl.multiple_of(begin + k * piece, piece), piece)
+
+    loads = [
+        pltpu.make_async_copy(up.at[0, 0], own_up, load_sem.at[0]),
+        pltpu.make_async_copy(down.at[0, 0], own_down, load_sem.at[1]),
+        pltpu.make_async_copy(pending.at[0], x.at[0, slot], load_sem.at[2]),
+    ]
+    arrivals = [
+        pltpu.make_async_copy(arriving.at[t], x.at[t + 1, slot], load_sem.at[3 + t])
+        for t in range(ticks - 1)
+    ]
+    for load in loads:
+        load.start()
+
+    @pl.when(first)
+    def _():
+        for load in arrivals:
+            load.start()
+
+    barrier = pltpu.get_barrier_semaphore()
+    for device in (mate, across, twin):
+        pl.semaphore_signal(barrier, inc=1, device_id=device, device_id_type=MESH)
+
+    @pl.when(has_ahead)
+    def _():
+        pl.semaphore_signal(barrier, inc=1, device_id=ahead, device_id_type=MESH)
+
+    @pl.when(has_behind)
+    def _():
+        pl.semaphore_signal(barrier, inc=1, device_id=behind, device_id_type=MESH)
+
+    pl.semaphore_wait(barrier, 3 + has_ahead.astype(jnp.int32) + has_behind.astype(jnp.int32))
+
+    route_copy = remote(routes, ids, x_sem, (0,), mate)
+    token_copy = remote(pending.at[0], x.at[0, slot], x_sem, (1,), mate)
+    arrival_copies = [
+        remote(arriving.at[t], x.at[t + 1, slot], x_sem, (2 + t,), mate) for t in range(ticks - 1)
+    ]
+    route_copy.start()
+    token_copy.start()
+
+    sends, shares = [], []
+    for k in range(up_cut):
+        mine = up_rows(my_half, k)
+        sends.append(remote(up.at[0, 0, mine], far_up.at[mine], up_sem, (k,), across))
+        shares.append(remote(far_up.at[mine], far_up.at[mine], up_share_sem, (k,), twin))
+    for c in range(cut):
+        mine = (pl.ds(my_hid, hid_half), pl.ds(c * wide, wide))
+        sends.append(remote(down.at[(0, 0, *mine)], far_down.at[mine], down_sem, (c,), across))
+        shares.append(remote(far_down.at[mine], far_down.at[mine], down_share_sem, (c,), twin))
+    for send in sends[:IN_FLIGHT]:
+        send.start()
+
+    def take(k):
+        sends[k].wait_recv()
+        shares[k].start()
+        if k + IN_FLIGHT < len(sends):
+            sends[k].wait_send()
+            sends[k + IN_FLIGHT].start()
+
+    loads[2].wait()
+    route_copy.wait()
+    token_copy.wait()
+
+    @pl.when(first)
+    def _():
+        for copy in arrival_copies:
+            copy.start()
+
+    both = (2 * rows, width)
+    gains = gain[...]
+    columns = gating[0]
+
+    def owners(t):
+        mine, theirs = (
+            column_of(ref[t].astype(jnp.float32)) for ref in (routes, ids)
+        )
+        return jnp.concatenate(
+            [jnp.where(slot == 0, mine, theirs), jnp.where(slot == 0, theirs, mine)], axis=0
+        )
+
+    def prepare(t):
+        rows_f32 = x[t].reshape(both).astype(jnp.float32)
+        inv_rms = lax.rsqrt(jnp.mean(rows_f32 * rows_f32, axis=-1, keepdims=True) + 1e-06)
+        normed = (rows_f32 * inv_rms * gains).astype(jnp.bfloat16)
+        owner = owners(t)
+        logits = jnp.dot(normed, columns, preferred_element_type=jnp.float32)
+        names = lax.broadcasted_iota(jnp.int32, logits.shape, 1).astype(jnp.float32)
+        logit = jnp.sum(jnp.where(owner == names, logits, 0.0), axis=1, keepdims=True)
+        gate[...] = jax.nn.sigmoid(logit)
+        return normed, owner == own_expert.astype(jnp.float32)
+
+    def hidden_of(normed, weights, kept):
+        value = jnp.dot(normed, weights, preferred_element_type=jnp.float32)
+        return jnp.where(kept, jnp.maximum(value, 0.0), 0.0).astype(jnp.bfloat16)
+
+    def part_copy(t, c):
+        span = pl.ds(c * wide, wide)
+        if t + 1 < ticks:
+            here = (t, slice(None), slice(None), span)
+        else:
+            here = (t, 1 - slot, slice(None), span)
+        return remote(part.at[here], their_part.at[here], part_sem, (t, c), mate)
+
+    def relay_copy(t, c):
+        span = (slice(None), slice(None), pl.ds(c * wide, wide))
+        return remote(y_out.at[(t, *span)], x.at[(t + 1, *span)], relay_sem, (t, c), ahead)
+
+    def put_part(t, c, value):
+        part[t, :, :, c * wide : (c + 1) * wide] = value.astype(jnp.bfloat16).reshape(2, rows, wide)
+        part_copy(t, c).start()
+
+    def finish(t, c):
+        part_copy(t, c).wait_recv()
+        span = slice(c * wide, (c + 1) * wide)
+        if t + 1 < ticks:
+            summed = part[t, :, :, span].astype(jnp.float32) + their_part[
+                t, :, :, span
+            ].astype(jnp.float32)
+            summed = summed.astype(jnp.bfloat16).astype(jnp.float32)
+            gates = gate[...].reshape(2, rows, 1)
+            y_out[t, :, :, span] = (
+                x[t, :, :, span].astype(jnp.float32) + gates * summed
+            ).astype(jnp.bfloat16)
+
+            @pl.when(has_ahead)
+            def _():
+                relay_copy(t, c).start()
+
+            out[0, t, :, span] = y_out[t, slot, :, span]
+        else:
+            summed = part[t, slot, :, span].astype(jnp.float32) + their_part[
+                t, slot, :, span
+            ].astype(jnp.float32)
+            summed = summed.astype(jnp.bfloat16).astype(jnp.float32)
+            gates = gate[pl.ds(pl.multiple_of(slot * rows, rows), rows), :]
+            out[0, t, :, span] = (
+                x[t, slot, :, span].astype(jnp.float32) + gates * summed
+            ).astype(jnp.bfloat16)
+
+    normed, kept = prepare(0)
+    loads[0].wait()
+    hidden[:, :hid] = hidden_of(normed, own_up[...], kept)
+    loads[1].wait()
+    own_sum[...] = jnp.dot(hidden[:, :hid], own_down[...], preferred_element_type=jnp.float32)
+    for k in range(up_cut):
+        take(k)
+    for k in range(up_cut):
+        shares[k].wait_recv()
+    hidden[:, hid:] = hidden_of(normed, far_up[...], jnp.logical_not(kept))
+    take(up_cut)
+    for c in range(cut):
+        if c + 1 < cut:
+            take(up_cut + c + 1)
+        shares[up_cut + c].wait_recv()
+        span = slice(c * wide, (c + 1) * wide)
+        put_part(
+            0,
+            c,
+            own_sum[:, span]
+            + jnp.dot(hidden[:, hid:], far_down[:, span], preferred_element_type=jnp.float32),
+        )
+        if c > 0:
+            finish(0, c - 1)
+    finish(0, cut - 1)
+
+    for t in range(1, ticks):
+
+        @pl.when(first)
+        def _():
+            arrivals[t - 1].wait()
+            arrival_copies[t - 1].wait()
+
+        @pl.when(has_behind)
+        def _():
+            for c in range(cut):
+                relay_copy(t - 1, c).wait_recv()
+
+        normed, kept = prepare(t)
+        hidden[:, :hid] = hidden_of(normed, own_up[...], kept)
+        hidden[:, hid:] = hidden_of(normed, far_up[...], jnp.logical_not(kept))
+        for c in range(cut):
+            span = slice(c * wide, (c + 1) * wide)
+            put_part(
+                t,
+                c,
+                jnp.dot(hidden[:, :hid], own_down[:, span], preferred_element_type=jnp.float32)
+                + jnp.dot(hidden[:, hid:], far_down[:, span], preferred_element_type=jnp.float32),
+            )
+        for c in range(cut):
+            finish(t, c)
+
+    for k, send in enumerate(sends):
+        if k + IN_FLIGHT >= len(sends):
+            send.wait_send()
+    for share in shares:
+        share.wait_send()
+    for t in range(ticks):
+        for c in range(cut):
+            part_copy(t, c).wait_send()
+
+    @pl.when(has_ahead)
+    def _():
+        for t in range(ticks - 1):
+            for c in range(cut):
+                relay_copy(t, c).wait_send()
+
+
+def relay(
+    sections,
+    pending_microgroups,
+    arriving_microgroups,
+    expert_choice_grid,
+    rootmean_gain,
+    gating_columns,
+    up_projection_matrix,
+    down_projection_matrix,
+):
+    _, rows, width = pending_microgroups.shape
+    ticks = expert_choice_grid.shape[0]
+    hid = up_projection_matrix.shape[3]
+    cut, up_cut = width // 128, 3
+    vmem, anywhere = pl.BlockSpec(memory_space=pltpu.VMEM), pl.BlockSpec(memory_space=pl.ANY)
+    sems = pltpu.SemaphoreType.DMA
+    return pl.pallas_call(
+        functools.partial(relay_kernel, sections, cut),
+        out_shape=jax.ShapeDtypeStruct((1, ticks, rows, width), jnp.bfloat16),
+        in_specs=[anywhere, anywhere, vmem, vmem, vmem, anywhere, anywhere],
+        out_specs=vmem,
+        scratch_shapes=[
+            pltpu.VMEM((ticks, 2, rows, width), jnp.bfloat16),
+            pltpu.VMEM((ticks, 2, rows, width), jnp.bfloat16),
+            pltpu.VMEM((ticks, 2, rows, width), jnp.bfloat16),
+            pltpu.VMEM((ticks - 1, 2, rows, width), jnp.bfloat16),
+            pltpu.VMEM((ticks, 1, rows), jnp.int32),
+            pltpu.VMEM((width, hid), jnp.bfloat16),
+            pltpu.VMEM((hid, width), jnp.bfloat16),
+            pltpu.VMEM((width, hid), jnp.bfloat16),
+            pltpu.VMEM((hid, width), jnp.bfloat16),
+            pltpu.VMEM((2 * rows, width), jnp.float32),
+            pltpu.VMEM((2 * rows, 2 * hid), jnp.bfloat16),
+            pltpu.VMEM((2 * rows, 1), jnp.float32),
+            sems((2 + ticks,)),
+            sems((2, 1 + ticks)),
+            sems((2, up_cut)),
+            sems((2, up_cut)),
+            sems((2, cut)),
+            sems((2, cut)),
+            sems((2, ticks, cut)),
+            sems((2, ticks - 1, cut)),
+        ],
+        compiler_params=pltpu.CompilerParams(
+            collective_id=0, has_side_effects=True, vmem_limit_bytes=48 * 2**20
+        ),
+    )(
+        pending_microgroups,
+        arriving_microgroups,
+        expert_choice_grid,
+        rootmean_gain,
+        gating_columns,
+        up_projection_matrix,
+        down_projection_matrix,
+    )
+
+
 def solution(mesh):
     placed = (
         P("section", ("groups", "expert"), None),
@@ -111,8 +462,13 @@
         P("section", "expert", None, None),
         P("section", "expert", None, None),
     )
+    shape = dict(mesh.shape)
+    if shape["expert"] == 4 and shape["groups"] == 2:
+        form = functools.partial(relay, shape["section"])
+    else:
+        form = per_device
     return jax.shard_map(
-        per_device,
+        form,
         mesh=mesh,
         in_specs=placed,
         out_specs=P("section", None, ("groups", "expert"), None),

time: 163 us -> 94.4 us (0.58)
  Pallas kernels: 0 us -> 86.6 us
  blocking collectives: 81.6 us -> 0 us
  waiting for transfers between devices: 36.6 us -> 0 us
  matrix products: 19.6 us -> 0 us
  starting transfers between devices: 18.2 us -> 0 us
  local copies, waits for them, and re-layouts: 1.25 us -> 7.5 us
  other arithmetic: 4.56 us -> 0 us
    pallas_call x0 -> x1, Pallas kernels: none -> 86.6 us  [relay(): pl.pallas_call(functools.partial(relay_kernel, sections, cut), out_shape=...]
    all_to_all x3 -> x0, blocking collectives: 81.6 us -> none  [expert_layer(): lax.all_to_all(halves, 'expert', split_axis=0, concat_axis=0, tiled=True)]
    all_to_all x3 -> x0, waiting for transfers between devices: 34.5 us -> none  [expert_layer(): lax.all_to_all(summed, 'expert', split_axis=0, concat_axis=0, tiled=True)]
    dot_general x15 -> x0, matrix products: 19.6 us -> none  [the longest x6 16.3 us: half_output(): jnp.einsum('sih,hd->sid', hidden, down_projection_matrix, preferred_eleme...]
    all_to_all x3 -> x0, starting transfers between devices: 11.5 us -> none  [expert_layer(): lax.all_to_all(summed, 'expert', split_axis=0, concat_axis=0, tiled=True)]
    unnamed x10 -> x14, local copies, waits for them, and re-layouts: 0.02 us -> 7.5 us
    ppermute x4 -> x0, starting transfers between devices: 6.73 us -> none  [the longest x2 3.62 us: from_behind(): lax.ppermute(value, axis, [(source, source + steps) for source in range(i...]
    ppermute x4 -> x0, waiting for transfers between devices: 2.08 us -> none  [the longest x2 2.08 us: from_behind(): lax.ppermute(value, axis, [(source, source + steps) for source in range(i...]
  transfers between devices with their start and end apart: 7 -> 0, of which waited for: 5 -> 0; matrix products, arithmetic and copies ran while one was open for 5% -> 0% of each run, Pallas kernels for 0% -> 0%
where the time goes in v1:
time: 94.4 us; the launch traced here: 94.1 us
  Pallas kernels  86.6 us (92%)
  local copies, waits for them, and re-layouts  7.5 us (8%)
    pallas_call x1, Pallas kernels, relay(): pl.pallas_call(functools.partial(relay_kernel, sections, cut), out_shape=...  86.6 us
    unnamed x14, local copies, waits for them, and re-layouts  7.5 us

profile of v1, /device:TPU:0, one launch (start us, length us, event | category | flops | bytes accessed | tf_op | source)
XLA Modules:
  0.0 94.1 jit_solution(4994528155946340430)
XLA Ops:
  0.0 0.9 copy.8.gating
  0.9 0.0 copy-start
  0.9 1.3 %copy-done = bf16[1,1,768,768]{3,2,1,0:T(8,128)(2,1)S(1)} copy-done((bf16[1,1,768,768]{3,2,1,0:T(8,128)(2,1)S(1)}, bf16[1,1,768,768]{3,2,1,0:T(8,128)(2,1)}, u32[]{:S(2)}) %copy-start) | copy-done | bytes 1179672
  2.1 0.0 copy-start.1
  2.1 1.3 %copy-done.1 = bf16[1,1,768,768]{3,2,1,0:T(8,128)(2,1)S(1)} copy-done((bf16[1,1,768,768]{3,2,1,0:T(8,128)(2,1)S(1)}, bf16[1,1,768,768]{3,2,1,0:T(8,128)(2,1)}, u32[]{:S(2)}) %copy-start.1) | copy-done | bytes 1179672
  3.4 0.0 copy-start.2
  3.4 1.0 %copy-done.2 = bf16[2,128,768]{2,1,0:T(8,128)(2,1)S(1)} copy-done((bf16[2,128,768]{2,1,0:T(8,128)(2,1)S(1)}, bf16[2,128,768]{2,1,0:T(8,128)(2,1)}, u32[]{:S(2)}) %copy-start.2) | copy-done | bytes 393240
  4.4 0.0 copy-start.3
  4.4 0.9 copy-done.3
  5.3 0.0 copy-start.4
  5.3 0.7 copy-done.4
  6.0 0.0 copy-start.5
  6.0 0.7 copy-done.5
  6.7 86.6 %shard_map.73 = bf16[1,3,128,768]{3,2,1,0:T(8,128)(2,1)S(1)} custom-call(bf16[1,128,768]{2,1,0:T(8,128)(2,1)S(1)} %copy-done.3, bf16[2,128,768]{2,1,0:T(8,128)(2,1)S(1)} %copy-done.2, s32[3,1,128]{2,1,0:T(1,128)S(1)} %copy-done.5, f32[1,768]{1,0:T(1,128)S(1)} %copy-done.4, bf16[1,768,2]{2,1,0:T(8,128)(2,1)S(1)} %copy.8.gating, ...), custom_call_target="tpu_custom_call" | custom-call | tf_op jit(solution)/shard_map/pallas_call | solution.py:414
  93.3 0.8 copy.10
Async XLA Ops:
  0.9 1.3 %copy-start = (bf16[1,1,768,768]{3,2,1,0:T(8,128)(2,1)S(1)}, bf16[1,1,768,768]{3,2,1,0:T(8,128)(2,1)}, u32[]{:S(2)}) copy-start(bf16[1,1,768,768]{3,2,1,0:T(8,128)(2,1)} %up.1) | copy-start | bytes 3538948
  2.1 1.3 %copy-start.1 = (bf16[1,1,768,768]{3,2,1,0:T(8,128)(2,1)S(1)}, bf16[1,1,768,768]{3,2,1,0:T(8,128)(2,1)}, u32[]{:S(2)}) copy-start(bf16[1,1,768,768]{3,2,1,0:T(8,128)(2,1)} %down.1) | copy-start | bytes 3538948
  3.4 1.0 %copy-start.2 = (bf16[2,128,768]{2,1,0:T(8,128)(2,1)S(1)}, bf16[2,128,768]{2,1,0:T(8,128)(2,1)}, u32[]{:S(2)}) copy-start(bf16[2,128,768]{2,1,0:T(8,128)(2,1)} %arriving.1) | copy-start | bytes 1179652
  4.4 0.9 copy-start.3
  5.3 0.7 copy-start.4
  6.0 0.7 copy-start.5

commit v2 on v1

--- a/solution.py
+++ b/solution.py
@@ -107,7 +107,7 @@
 
 
 MESH = pl.DeviceIdType.MESH
-IN_FLIGHT = 3
+IN_FLIGHT = 2
 
 
 def column_of(row):
@@ -273,7 +273,9 @@
         inv_rms = lax.rsqrt(jnp.mean(rows_f32 * rows_f32, axis=-1, keepdims=True) + 1e-06)
         normed = (rows_f32 * inv_rms * gains).astype(jnp.bfloat16)
         owner = owners(t)
-        logits = jnp.dot(normed, columns, preferred_element_type=jnp.float32)
+        logits = lax.dot_general(
+            normed, columns, (((1,), (1,)), ((), ())), preferred_element_type=jnp.float32
+        )
         names = lax.broadcasted_iota(jnp.int32, logits.shape, 1).astype(jnp.float32)
         logit = jnp.sum(jnp.where(owner == names, logits, 0.0), axis=1, keepdims=True)
         gate[...] = jax.nn.sigmoid(logit)
@@ -439,14 +441,14 @@
             sems((2, ticks - 1, cut)),
         ],
         compiler_params=pltpu.CompilerParams(
-            collective_id=0, has_side_effects=True, vmem_limit_bytes=48 * 2**20
+            collective_id=0, has_side_effects=True, vmem_limit_bytes=63 * 2**20
         ),
     )(
         pending_microgroups,
         arriving_microgroups,
         expert_choice_grid,
         rootmean_gain,
-        gating_columns,
+        jnp.swapaxes(gating_columns, 1, 2),
         up_projection_matrix,
         down_projection_matrix,
     )

time: 94.4 us -> 89.4 us (0.947)
  local copies, waits for them, and re-layouts: 7.5 us -> 1.92 us
    unnamed x14 -> x1, local copies, waits for them, and re-layouts: 7.5 us -> 1.92 us
where the time goes in v2:
time: 89.4 us; the launch traced here: 89.2 us
  Pallas kernels  87.3 us (98%)
  local copies, waits for them, and re-layouts  1.92 us (2%)
    pallas_call x1, Pallas kernels, relay(): pl.pallas_call(functools.partial(relay_kernel, sections, cut), out_shape=...  87.3 us
    unnamed x1, local copies, waits for them, and re-layouts  1.92 us

profile of v2, /device:TPU:0, one launch (start us, length us, event | category | flops | bytes accessed | tf_op | source)
XLA Modules:
  0.0 89.2 jit_solution(1749493812440374315)
XLA Ops:
  0.0 87.3 %shard_map.73 = bf16[1,3,128,768]{3,2,1,0:T(8,128)(2,1)} custom-call(bf16[1,128,768]{2,1,0:T(8,128)(2,1)} %pending.1, bf16[2,128,768]{2,1,0:T(8,128)(2,1)} %arriving.1, s32[3,1,128]{2,1,0:T(1,128)} %routes.1, f32[1,768]{1,0:T(1,128)} %gain.1, bf16[1,2,768]{2,1,0:T(2,128)(2,1)} %bitcast.1, bf16[1,1,768,768]{3,2,1,0:T(8,128)(2,1)} %up.1, ...), custom_call_target="tpu_custom_call" | custom-call | tf_op jit(solution)/shard_map/pallas_call | solution.py:416
  87.3 1.9 %copy.9 = bf16[1,3,128,768]{3,2,1,0:T(8,128)(2,1)} copy(bf16[1,3,128,768]{3,2,1,0:T(8,128)(2,1)} %shard_map.73) | data formatting | bytes 1179648
